TPU v7x, 512 devices: a whole 4x8x8 slice. The times are simulated.
512 devices in a mesh: rows: 32 (over x, y), tp: 16 (over z, core).
Axes of the slice: x: 4, y: 8, z: 8, core: 2. Of those that a mesh axis runs over, the one named last changes fastest.
Arguments:
- queries: bfloat16 [8192, 8192], P('rows', 'tp'), may hold values from -32 to 32
- nbr_keys: bfloat16 [32768, 8192], P(('rows', 'tp')), may hold values from -8 to 8
- nbr_values: bfloat16 [32768, 8192], P(('rows', 'tp')), may hold values from -15 to 15
- nbr_index: int32 [128, 2], P('rows'), may hold values from 0 to 7, all different within a row
- residual: bfloat16 [8192, 8192], P(('rows', 'tp')), may hold values from -2 to 2
- out_weight: bfloat16 [8192, 8192], P('tp', 'rows'), may hold values from -0.0625 to 0.0625
Outputs:
- mixed: bfloat16 [8192, 8192], P(('rows', 'tp'))
Inputs may be any that keep to these rules, and one draw needn't show every extreme that they name: `nbr_index`: the 2 entries of a span differ; they index the 8 neighbours retrieved for that span's own sequence shard.
All inputs are finite; a program needn't handle non-finite values.
Results may differ from a plain program's by a relative error of at most 0.022.
Values may be sent and summed in bfloat16 or wider, within the bound.
A program may use at most 64 MiB of HBM per device.

v0:
```python
import math

import jax
import jax.numpy as jnp
from jax import lax
from jax.sharding import PartitionSpec as P

HD = 128
CH = 64
R = 128


def shards(queries, nbr_keys, nbr_values, nbr_index, residual, out_weight):
    keys_local, values_local = (
        lax.all_to_all(nbr_keys, "tp", split_axis=1, concat_axis=0, tiled=True),
        lax.all_to_all(nbr_values, "tp", split_axis=1, concat_axis=0, tiled=True),
    )
    heads_local = queries.shape[1] // HD
    span_count = queries.shape[0] // CH
    neighbour_count = keys_local.shape[0] // R
    score_scale = 1.0 / math.sqrt(HD)
    query_blocks = queries.reshape(span_count, CH, heads_local, HD)
    key_blocks = keys_local.reshape(neighbour_count, R, heads_local, HD)[nbr_index]
    value_blocks = values_local.reshape(neighbour_count, R, heads_local, HD)[nbr_index]
    scores = (
        jnp.einsum(
            "cqhd,ckrhd->chqkr", query_blocks, key_blocks, preferred_element_type=jnp.float32
        )
        * score_scale
    )
    row_top = jnp.max(scores, axis=(3, 4), keepdims=True)
    weights = jnp.exp(scores - row_top)
    probs = (weights / jnp.sum(weights, axis=(3, 4), keepdims=True)).astype(jnp.bfloat16)
    attended = jnp.einsum(
        "chqkr,ckrhd->cqhd", probs, value_blocks, preferred_element_type=jnp.float32
    )
    attn = attended.astype(jnp.bfloat16).reshape(queries.shape[0], heads_local * HD)
    partial_value = jnp.dot(
        attn,
        lax.all_gather(out_weight, "rows", axis=1, tiled=True),
        preferred_element_type=jnp.float32,
    )
    summed = lax.psum_scatter(
        partial_value.astype(jnp.bfloat16), "tp", scatter_dimension=0, tiled=True
    ).astype(jnp.float32)
    return (residual.astype(jnp.float32) + summed).astype(jnp.bfloat16)


def solution(mesh):
    placed = (
        P("rows", "tp"),
        P(("rows", "tp"), None),
        P(("rows", "tp"), None),
        P("rows", None),
        P(("rows", "tp"), None),
        P("tp", "rows"),
    )
    return jax.shard_map(
        shards, mesh=mesh, in_specs=placed, out_specs=P(("rows", "tp"), None), check_vma=False
    )
```

profile of v0, /device:TPU:1, one launch (start us, length us, event | category | flops | bytes accessed | tf_op | source)
XLA Modules:
  0.0 202.6 jit_solution(4204165510992683133)
XLA Ops:
  6.5 0.0 copy-start.3
  6.5 0.0 copy-start.2
  6.5 0.0 all-gather.2.cloned.1.call-start
  6.5 0.7 all-gather.2.cloned.1.call-update
  7.3 2.3 %copy.46 = bf16[8,16,8,512]{3,2,0,1:T(8,128)(2,1)} copy(bf16[8,16,8,512]{3,2,1,0:T(8,128)(2,1)} %bitcast.35) | data formatting | bytes 2097152 | tf_op jit(solution)/shard_map/all_to_all | solution.py:15
  9.6 11.8 %all-to-all-start.1 = ((bf16[64,16,512]{2,0,1:T(8,128)(2,1)}), bf16[64,16,512]{2,0,1:T(8,128)(2,1)S(1)}, u32[]{:S(2)}, u32[]{:S(2)}) async-start(bf16[64,16,512]{2,0,1:T(8,128)(2,1)} %bitcast.29), calls=%async_computation.1 | async-start | bytes 2097152 | tf_op jit(solution)/shard_map/all_to_all | solution.py:15
  21.4 2.4 %copy.45 = bf16[8,16,8,512]{3,2,0,1:T(8,128)(2,1)} copy(bf16[8,16,8,512]{3,2,1,0:T(8,128)(2,1)} %bitcast.36) | data formatting | bytes 2097152 | tf_op jit(solution)/shard_map/all_to_all | solution.py:16
  23.8 25.5 %all-to-all-done.1 = bf16[64,16,512]{2,0,1:T(8,128)(2,1)S(1)} async-done(((bf16[64,16,512]{2,0,1:T(8,128)(2,1)}), bf16[64,16,512]{2,0,1:T(8,128)(2,1)S(1)}, u32[]{:S(2)}, u32[]{:S(2)}) %all-to-all-start.1) | async-done | bytes 1048608 | tf_op jit(solution)/shard_map/all_to_all | solution.py:15
  49.3 3.6 %all-to-all-start = ((bf16[64,16,512]{2,0,1:T(8,128)(2,1)}), bf16[64,16,512]{2,0,1:T(8,128)(2,1)S(1)}, u32[]{:S(2)}, u32[]{:S(2)}) async-start(bf16[64,16,512]{2,0,1:T(8,128)(2,1)} %bitcast.28), calls=%async_computation | async-start | bytes 2097152 | tf_op jit(solution)/shard_map/all_to_all | solution.py:16
  52.9 0.0 reduce-scatter.2.cloned.1.call-start
  52.9 0.0 copy-done.3
  53.0 0.1 copy.10
  53.1 0.1 reshape.28
  53.1 0.0 copy-done.2
  53.1 0.1 reshape.24
  53.2 0.3 reshape.23
  53.5 27.3 %all-to-all-done = bf16[64,16,512]{2,0,1:T(8,128)(2,1)S(1)} async-done(((bf16[64,16,512]{2,0,1:T(8,128)(2,1)}), bf16[64,16,512]{2,0,1:T(8,128)(2,1)S(1)}, u32[]{:S(2)}, u32[]{:S(2)}) %all-to-all-start) | async-done | bytes 1048608 | tf_op jit(solution)/shard_map/all_to_all | solution.py:16
  80.8 0.0 copy-start
  80.8 1.0 copy-done
  81.8 1.3 reshape.22
  83.2 1.4 gather_fusion.1
  84.6 1.4 gather_fusion
  86.1 0.6 fusion.11
  86.7 0.4 fusion.5
  87.1 0.5 fusion.2
  87.6 0.2 copy.17
  87.8 34.5 %all-gather.2.cloned.1.call-done = bf16[512,8192]{1,0:T(8,128)(2,1)} async-done(((bf16[512,256]{1,0:T(8,128)(2,1)}), bf16[512,8192]{1,0:T(8,128)(2,1)}) %all-gather.2.cloned.1.call-update) | async-done | bytes 8388624 | tf_op jit(solution)/shard_map/all_gather | solution.py:40
  122.3 7.7 %convolution_convert_fusion = bf16[256,8192]{1,0:T(8,128)(2,1)} fusion(bf16[512,8192]{1,0:T(8,128)(2,1)} %all-gather.2.cloned.1.call-done, bf16[32,8,4,128]{3,2,1,0:T(4,128)(2,1)S(1)} %bitcast.37), kind=kOutput, calls=%fused_computation.2 | convolution fusion | flops 2149580800 | bytes 12845056 | tf_op jit(solution)/shard_map/dot_general | solution.py:38
  130.1 0.0 reduce-scatter.2.cloned.1.call-update
  130.1 63.9 %reduce-scatter.2.cloned.1.call-done = bf16[16,8192]{1,0:T(8,128)(2,1)} async-done(((bf16[256,8192]{1,0:T(8,128)(2,1)}), bf16[16,8192]{1,0:T(8,128)(2,1)}) %reduce-scatter.2.cloned.1.call-update) | async-done | bytes 262160 | tf_op jit(solution)/shard_map/reduce_scatter | solution.py:43
  194.0 0.0 copy-done.1
  194.0 1.7 add_convert_fusion
  (3 shorter events, 0.0 us)
Async XLA Ops:
  6.5 46.4 %copy-start.3 = (s32[4,2]{0,1:T(2,128)S(1)}, s32[4,2]{0,1:T(2,128)}, u32[]{:S(2)}) copy-start(s32[4,2]{0,1:T(2,128)} %param.9) | copy-start | bytes 100
  6.5 46.6 %copy-start.2 = (bf16[256,512]{1,0:T(8,128)(2,1)S(1)}, bf16[256,512]{1,0:T(8,128)(2,1)}, u32[]{:S(2)}) copy-start(bf16[256,512]{1,0:T(8,128)(2,1)} %param.6) | copy-start | bytes 786436
  6.5 115.8 %all-gather.2.cloned.1.call-start = ((), (), s32[]{:S(2)}) async-start(), calls=%async_computation.3 | async-start | bytes 8650752 | tf_op jit(solution)/shard_map/all_gather | solution.py:40
  9.6 39.8 %all-to-all-start.1 = ((bf16[64,16,512]{2,0,1:T(8,128)(2,1)}), bf16[64,16,512]{2,0,1:T(8,128)(2,1)S(1)}, u32[]{:S(2)}, u32[]{:S(2)}) async-start(bf16[64,16,512]{2,0,1:T(8,128)(2,1)} %bitcast.29), calls=%async_computation.1 | async-start | bytes 2097152 | tf_op jit(solution)/shard_map/all_to_all | solution.py:15
  49.3 31.5 %all-to-all-start = ((bf16[64,16,512]{2,0,1:T(8,128)(2,1)}), bf16[64,16,512]{2,0,1:T(8,128)(2,1)S(1)}, u32[]{:S(2)}, u32[]{:S(2)}) async-start(bf16[64,16,512]{2,0,1:T(8,128)(2,1)} %bitcast.28), calls=%async_computation | async-start | bytes 2097152 | tf_op jit(solution)/shard_map/all_to_all | solution.py:16
  52.9 141.2 %reduce-scatter.2.cloned.1.call-start = ((), (), s32[]{:S(2)}) async-start(), calls=%async_computation.4 | async-start | bytes 4456448 | tf_op jit(solution)/shard_map/reduce_scatter | solution.py:43
  80.8 1.1 copy-start
  122.3 71.7 %copy-start.1 = (bf16[16,8192]{1,0:T(8,128)(2,1)S(1)}, bf16[16,8192]{1,0:T(8,128)(2,1)}, u32[]{:S(2)}) copy-start(bf16[16,8192]{1,0:T(8,128)(2,1)} %param.10) | copy-start | bytes 786436
Sparse Core Ops, SparseCore 0:
  10.4 111.8 all-gather.1
  130.2 63.7 reduce-scatter.1
where the time goes:
time: 205 us; the launch traced here: 203 us
  waiting for transfers between devices  152 us (74%)
  starting transfers between devices  15.4 us (8%)
  between operations  13.5 us (7%)
  local copies, waits for them, and re-layouts  10.7 us (5%)
  matrix products  8.81 us (4%)
  other arithmetic  2.14 us (1%)
    reduce_scatter x1, waiting for transfers between devices, shards(): lax.psum_scatter(partial_value.astype(jnp.bfloat16), 'tp', scatter_dimens...  63.9 us
    all_gather x1, waiting for transfers between devices, shards(): lax.all_gather(out_weight, 'rows', axis=1, tiled=True)  34.5 us
    all_to_all x1, waiting for transfers between devices, shards(): lax.all_to_all(nbr_values, 'tp', split_axis=1, concat_axis=0, tiled=True)  27.3 us
    all_to_all x1, waiting for transfers between devices, shards(): lax.all_to_all(nbr_keys, 'tp', split_axis=1, concat_axis=0, tiled=True)  25.5 us
    all_to_all x1, starting transfers between devices, shards(): lax.all_to_all(nbr_keys, 'tp', split_axis=1, concat_axis=0, tiled=True)  11.8 us
    dot_general x1, matrix products, shards(): jnp.dot(attn, lax.all_gather(out_weight, 'rows', axis=1, tiled=True), pre...  7.74 us
  transfers between devices with their start and end apart: 4, of which 4 were waited for; matrix products, arithmetic and copies ran while one was open for 6% of the time, Pallas kernels for 0%

commit v1 on v0

v1 whole, which is shorter than its diff:
```python
import functools
import heapq
import math

import jax
import jax.numpy as jnp
from jax import lax
from jax.experimental import pallas as pl
from jax.experimental.pallas import tpu as pltpu
from jax.sharding import PartitionSpec as P

MESH = pl.DeviceIdType.MESH
F32, BF16 = jnp.float32, jnp.bfloat16

HD, CH, R = 128, 64, 128
NX, NY, NZ = 4, 8, 8
TP, ROWS = 16, 32
TOK, HCOLS, WCOLS, KROWS = 256, 512, 256, 64
D = 8192
SPANS, HEADS = TOK // CH, HCOLS // HD
TOKZ, TOKD = TOK // NZ, TOK // TP
HALF = D // 2
G = 4
GC = HALF // G
GB = GC // WCOLS

PARTS = ((0, 208, 112), (208, 512, 352))


def gather_plan():
    messages, needs = [], []

    def add(part, axis, sign, dx, dy, piece, need):
        lo, hi, mid = PARTS[part]
        lo, hi = ((lo, hi), (lo, mid), (mid, hi))[piece]
        messages.append((axis, sign, dx, dy, lo, hi))
        needs.append(need)
        return len(messages) - 1

    def ring(part, axis, size, other, need):
        got = {0: need}
        for sign in (1, -1):
            for step in range(size // 2):
                at = -sign * step
                last = step == size // 2 - 1
                piece = 0 if not last else (1 if sign == 1 else 2)
                dx, dy = (at, other) if axis == 0 else (other, at)
                bring = add(part, axis, sign, dx, dy, piece, got[at])
                key = size // 2 if last else at - sign
                got[key] = got.get(key, ()) + (bring,) if last else (bring,)
        return got

    for bx, need in ring(0, 0, NX, 0, ()).items():
        ring(0, 1, NY, bx, need)
    for by, need in ring(1, 1, NY, 0, ()).items():
        ring(1, 0, NX, by, need)

    count = len(messages)
    feeds = [[j for j in range(count) if i in needs[j]] for i in range(count)]
    depth = [0] * count
    for i in reversed(range(count)):
        depth[i] = max([1 + depth[j] for j in feeds[i]], default=0)
    rate, delay = 2 * WCOLS * 2 / 90e3, 1.5
    free = {}
    queue = []
    left = [len(n) for n in needs]

    def launch(i, now):
        axis, sign, _, _, lo, hi = messages[i]
        begin = max(now, free.get((axis, sign), 0.0))
        free[axis, sign] = begin + (hi - lo) * rate
        heapq.heappush(queue, (free[axis, sign] + delay, i))

    first = sorted((i for i in range(count) if not needs[i]), key=lambda i: (-depth[i], i))
    for i in first:
        launch(i, 0.0)
    steps = []
    while queue:
        now, i = heapq.heappop(queue)
        ready = []
        for j in feeds[i]:
            left[j] -= 1
            if left[j] == 0:
                ready.append(j)
        ready.sort(key=lambda j: (-depth[j], j))
        for j in ready:
            launch(j, now)
        steps.append((now, i, ready, not feeds[i]))
    return messages, first, steps


MESSAGES, FIRST, STEPS = gather_plan()


def kernel(
    do_kv, do_w, do_rs, score_at,
    idx_ref, q_ref, k_ref, v_ref, res_ref, w_ref, out_ref,
    kbuf, vbuf, qbuf, rbuf, wbuf, attn, probs, xsend, xrecv, pown, sbuf, rplus, rminus, fin,
    local_sem, kv_send, kv_recv, w_send, w_recv, r_send, r_recv, x_send, x_recv, c_send, c_recv, f_send, f_recv,
):
    row, tp = lax.axis_index("rows"), lax.axis_index("tp")
    x, y = row // NY, row % NY
    z, core = tp // 2, tp % 2
    sibling = z * 2 + (1 - core)

    def at_z(dz, dc=0):
        return ((z + dz) % NZ) * 2 + (core + dc) % 2

    def at_xy(axis, sign):
        if axis == 0:
            return ((x + sign) % NX) * NY + y
        return x * NY + (y + sign) % NY

    partners = [(row, sibling)]
    partners += [(row, at_z(dz, dc)) for dz in (4, 3, -3, 2, -2, 1, -1) for dc in (0, 1)]
    around = [(at_xy(axis, sign), tp) for axis in (0, 1) for sign in (1, -1)]

    barrier = pltpu.get_barrier_semaphore()
    for who in partners + around:
        pl.semaphore_signal(barrier, inc=1, device_id=who, device_id_type=MESH)

    own = (z, pl.ds(pl.multiple_of(core * KROWS, KROWS), KROWS))
    own_cols = pl.multiple_of(tp * HCOLS, HCOLS)
    my_half = pl.multiple_of(core * HALF, HALF)
    its_half = pl.multiple_of((1 - core) * HALF, HALF)
    my_rows = pl.ds(pl.multiple_of(core * TOKD, TOKD), TOKD)
    its_rows = pl.ds(pl.multiple_of((1 - core) * TOKD, TOKD), TOKD)

    locals_ = [
        pltpu.make_async_copy(q_ref, qbuf, local_sem.at[0]),
        pltpu.make_async_copy(k_ref.at[:, pl.ds(own_cols, HCOLS)], kbuf.at[own], kv_recv.at[0]),
        pltpu.make_async_copy(v_ref.at[:, pl.ds(own_cols, HCOLS)], vbuf.at[own], kv_recv.at[1]),
        pltpu.make_async_copy(w_ref, wbuf.at[row], local_sem.at[3]),
        pltpu.make_async_copy(res_ref.at[:, pl.ds(my_half, HALF)], rbuf.at[my_rows], local_sem.at[4]),
    ]
    for copy in locals_:
        copy.start()
    pl.semaphore_wait(barrier, len(partners) + len(around))

    def owner(dx, dy):
        return ((x + dx) % NX) * NY + (y + dy) % NY

    def w_copy(i, arrived):
        axis, sign, dx, dy, lo, hi = MESSAGES[i]
        if arrived:
            dx, dy = (dx - sign, dy) if axis == 0 else (dx, dy - sign)
        slot = wbuf.at[owner(dx, dy), pl.ds(lo, hi - lo), :]
        mine = not arrived and dx == 0 and dy == 0
        return pltpu.make_async_remote_copy(
            src_ref=w_ref.at[pl.ds(lo, hi - lo), :] if mine else slot,
            dst_ref=slot,
            send_sem=w_send,
            recv_sem=w_recv.at[i],
            device_id=(at_xy(axis, sign), tp),
            device_id_type=MESH,
        )

    if do_w:
        for i in FIRST:
            w_copy(i, False).start()
    if do_kv:
        for which, (src, dst) in enumerate(((k_ref, kbuf), (v_ref, vbuf))):
            for _, to in partners[1:] + partners[:1]:
                pltpu.make_async_remote_copy(
                    src_ref=src.at[:, pl.ds(pl.multiple_of(to * HCOLS, HCOLS), HCOLS)],
                    dst_ref=dst.at[own],
                    send_sem=kv_send.at[which],
                    recv_sem=kv_recv.at[which],
                    device_id=(row, to),
                    device_id_type=MESH,
                ).start()
    residual_copy = pltpu.make_async_remote_copy(
        src_ref=res_ref.at[:, pl.ds(its_half, HALF)],
        dst_ref=rbuf.at[my_rows],
        send_sem=r_send,
        recv_sem=r_recv,
        device_id=(row, sibling),
        device_id_type=MESH,
    )
    residual_copy.start()

    def kv_wait(which):
        buf = (kbuf, vbuf)[which]
        if do_kv:
            pltpu.make_async_copy(buf, buf, kv_recv.at[which]).wait()
        else:
            locals_[1 + which].wait()

    def score(span):
        rows = pl.ds(span * CH, CH)
        keys = [kbuf[idx_ref[span, k]] for k in range(2)]
        for h in range(HEADS):
            query = qbuf[rows, h * HD:(h + 1) * HD]
            raw = jnp.concatenate(
                [
                    lax.dot_general(
                        query, block[:, h * HD:(h + 1) * HD], (((1,), (1,)), ((), ())),
                        preferred_element_type=F32,
                    )
                    for block in keys
                ],
                axis=1,
            ) * (1.0 / math.sqrt(HD))
            weights = jnp.exp(raw - jnp.max(raw, axis=1, keepdims=True))
            total = jnp.sum(weights, axis=1, keepdims=True)
            probs[rows, h * 2 * R:(h + 1) * 2 * R] = (weights / total).astype(BF16)

    def attend(span):
        rows = pl.ds(span * CH, CH)
        values = [vbuf[idx_ref[span, k]] for k in range(2)]
        for h in range(HEADS):
            value = jnp.concatenate([block[:, h * HD:(h + 1) * HD] for block in values], axis=0)
            out = jnp.dot(probs[rows, h * 2 * R:(h + 1) * 2 * R], value, preferred_element_type=F32)
            attn[rows, h * HD:(h + 1) * HD] = out.astype(BF16)

    locals_[0].wait()
    scored = False
    late = []
    if do_w:
        for now, i, sends, last in STEPS:
            if now > score_at and not scored:
                scored = True
                kv_wait(0)
                for span in range(SPANS):
                    score(span)
            if last:
                late.append(i)
                continue
            w_copy(i, True).wait_recv()
            for j in sends:
                w_copy(j, False).start()
    if not scored:
        kv_wait(0)
        for span in range(SPANS):
            score(span)
    kv_wait(1)
    for span in range(SPANS):
        attend(span)
    for i in late:
        w_copy(i, True).wait_recv()
    for copy in locals_[3:]:
        copy.wait()
    residual_copy.wait()

    def chain(g, step, sign):
        buf = rplus if sign == 1 else rminus
        way = 0 if sign == 1 else 1
        if step == 0:
            tokens = pl.ds(pl.multiple_of(((z + 4) % NZ) * TOKZ, TOKZ), TOKZ)
            cols = pl.ds(way * (GC // 2), GC // 2)
            src, dst = sbuf.at[g, tokens, cols], buf.at[g, 0, :, cols]
        else:
            src, dst = buf.at[g, step - 1], buf.at[g, step]
        return pltpu.make_async_remote_copy(
            src_ref=src,
            dst_ref=dst,
            send_sem=c_send.at[way, g, step],
            recv_sem=c_recv.at[way, g, step],
            device_id=(row, at_z(sign)),
            device_id_type=MESH,
        )

    def tokens_of(dz):
        return pl.ds(pl.multiple_of(((z + dz) % NZ) * TOKZ, TOKZ), TOKZ)

    def exchange(g):
        return pltpu.make_async_remote_copy(
            src_ref=xsend.at[g],
            dst_ref=xrecv.at[g],
            send_sem=x_send.at[g],
            recv_sem=x_recv.at[g],
            device_id=(row, sibling),
            device_id_type=MESH,
        )

    def project(g):
        for side in (1 - core, core):
            for j in range(GB):
                block = wbuf[side * (ROWS // 2) + g * GB + j]
                part = jnp.dot(attn[...], block, preferred_element_type=F32)
                cols = slice(j * WCOLS, (j + 1) * WCOLS)
                if side is core:
                    pown[g, :, cols] = part
                else:
                    xsend[g, :, cols] = part.astype(BF16)
            if side is not core:
                exchange(g).start()

    def combine(g):
        exchange(g).wait_recv()
        sbuf[g] = (pown[g] + xrecv[g].astype(F32)).astype(BF16)
        for sign in (1, -1):
            chain(g, 0, sign).start()

    def relay(g, step):
        for sign in (1, -1):
            buf = rplus if sign == 1 else rminus
            chain(g, step - 1, sign).wait_recv()
            tokens = tokens_of(sign * (4 - step))
            if step == 1:
                cut = GC // 2
                got, rest = (slice(0, cut), slice(cut, GC)) if sign == 1 else (slice(cut, GC), slice(0, cut))
                buf[g, 0, :, got] = (buf[g, 0, :, got].astype(F32) + sbuf[g, tokens, got].astype(F32)).astype(BF16)
                buf[g, 0, :, rest] = sbuf[g, tokens, rest]
            else:
                buf[g, step - 1] = (buf[g, step - 1].astype(F32) + sbuf[g, tokens, :].astype(F32)).astype(BF16)
            chain(g, step, sign).start()

    def final_copy(g, cols):
        return pltpu.make_async_remote_copy(
            src_ref=fin.at[g],
            dst_ref=out_ref.at[:, cols],
            send_sem=f_send.at[g],
            recv_sem=f_recv.at[g],
            device_id=(row, sibling),
            device_id_type=MESH,
        )

    def finish(g):
        for sign in (1, -1):
            chain(g, 3, sign).wait_recv()
        cols = pl.ds(g * GC, GC)
        for rows, base in ((its_rows, (1 - core) * TOKD), (my_rows, core * TOKD)):
            tokens = pl.ds(pl.multiple_of(z * TOKZ + base, TOKD), TOKD)
            total = (
                rbuf[rows, cols].astype(F32)
                + sbuf[g, tokens, :].astype(F32)
                + rplus[g, 3, rows, :].astype(F32)
                + rminus[g, 3, rows, :].astype(F32)
            ).astype(BF16)
            if rows is its_rows:
                fin[g] = total
                final_copy(g, pl.ds(pl.multiple_of(my_half + g * GC, GC), GC)).start()
            else:
                out_ref[:, pl.ds(pl.multiple_of(my_half + g * GC, GC), GC)] = total

    if do_rs:
        for wave in range(G + 5):
            if wave < G:
                project(wave)
            for step in range(5):
                g = wave - 1 - step
                if 0 <= g < G:
                    if step == 0:
                        combine(g)
                    elif step < 4:
                        relay(g, step)
                    else:
                        finish(g)
        for g in range(G):
            final_copy(g, pl.ds(pl.multiple_of(its_half + g * GC, GC), GC)).wait_recv()
        for g in range(G):
            exchange(g).wait_send()
            final_copy(g, pl.ds(pl.multiple_of(my_half + g * GC, GC), GC)).wait_send()
            for step in range(4):
                for sign in (1, -1):
                    chain(g, step, sign).wait_send()
    else:
        out_ref[...] = jnp.zeros_like(out_ref)
        out_ref[:, 0:HCOLS] = attn[0:TOKD, :]
    if do_kv:
        waitbuf = wbuf.at[pl.ds(0, TP - 1), pl.ds(0, KROWS * HCOLS // WCOLS), :]
        for which in range(2):
            pltpu.make_async_copy(waitbuf, waitbuf, kv_send.at[which]).wait()
    if do_w:
        rest = wbuf.at[pl.ds(0, ROWS - 1)]
        pltpu.make_async_copy(rest, rest, w_send).wait()


def build(mesh, do_kv=True, do_w=True, do_rs=True, score_at=30.0, collective_id=0):
    def shards(queries, nbr_keys, nbr_values, nbr_index, residual, out_weight):
        hbm = pl.BlockSpec(memory_space=pl.ANY)
        dma = pltpu.SemaphoreType.DMA
        return pl.pallas_call(
            functools.partial(kernel, do_kv, do_w, do_rs, score_at),
            out_shape=jax.ShapeDtypeStruct((TOKD, D), BF16),
            in_specs=[pl.BlockSpec(memory_space=pltpu.SMEM)] + [hbm] * 5,
            out_specs=pl.BlockSpec(memory_space=pltpu.VMEM),
            scratch_shapes=[
                pltpu.VMEM((NZ, R, HCOLS), BF16),
                pltpu.VMEM((NZ, R, HCOLS), BF16),
                pltpu.VMEM((TOK, HCOLS), BF16),
                pltpu.VMEM((TOKZ, HALF), BF16),
                pltpu.VMEM((ROWS, HCOLS, WCOLS), BF16),
                pltpu.VMEM((TOK, HCOLS), BF16),
                pltpu.VMEM((TOK, HEADS * 2 * R), BF16),
                pltpu.VMEM((G, TOK, GC), BF16),
                pltpu.VMEM((G, TOK, GC), BF16),
                pltpu.VMEM((G, TOK, GC), F32),
                pltpu.VMEM((G, TOK, GC), BF16),
                pltpu.VMEM((G, 4, TOKZ, GC), BF16),
                pltpu.VMEM((G, 4, TOKZ, GC), BF16),
                pltpu.VMEM((G, TOKD, GC), BF16),
                dma((5,)), dma((2,)), dma((2,)), dma, dma((len(MESSAGES),)), dma, dma,
                dma((G,)), dma((G,)), dma((2, G, 4)), dma((2, G, 4)), dma((G,)), dma((G,)),
            ],
            compiler_params=pltpu.CompilerParams(
                collective_id=collective_id, has_side_effects=True, vmem_limit_bytes=48 * 1024 * 1024
            ),
            cost_estimate=pl.CostEstimate(flops=2_400_000_000, bytes_accessed=12_000_000, transcendentals=262144),
        )(nbr_index, queries, nbr_keys, nbr_values, residual, out_weight)

    placed = (
        P("rows", "tp"),
        P(("rows", "tp"), None),
        P(("rows", "tp"), None),
        P("rows", None),
        P(("rows", "tp"), None),
        P("tp", "rows"),
    )
    return jax.shard_map(
        shards, mesh=mesh, in_specs=placed, out_specs=P(("rows", "tp"), None), check_vma=False
    )


def solution(mesh):
    return build(mesh)
```

time: 205 us -> 100 us (0.49); the launches traced: 203 us -> 100 us
  waiting for transfers between devices: 152 us -> 0 us
  Pallas kernels: 0 us -> 93.4 us
  starting transfers between devices: 15.4 us -> 0 us
  between operations: 13.5 us -> 0.01 us
  matrix products: 8.81 us -> 0 us
  local copies, waits for them, and re-layouts: 10.7 us -> 6.77 us
  other arithmetic: 2.14 us -> 0 us
    pallas_call x0 -> x1, Pallas kernels: none -> 93.4 us  [shards(): pl.pallas_call(functools.partial(kernel, do_kv, do_w, do_rs, score_at), o...]
    reduce_scatter x1 -> x0, waiting for transfers between devices: 63.9 us -> none  [shards(): lax.psum_scatter(partial_value.astype(jnp.bfloat16), 'tp', scatter_dimens...]
    all_to_all x2 -> x0, waiting for transfers between devices: 52.8 us -> none  [the longest x1 27.3 us: shards(): lax.all_to_all(nbr_values, 'tp', split_axis=1, concat_axis=0, tiled=True)]
    all_gather x1 -> x0, waiting for transfers between devices: 34.5 us -> none  [shards(): lax.all_gather(out_weight, 'rows', axis=1, tiled=True)]
    all_to_all x2 -> x0, starting transfers between devices: 15.4 us -> none  [the longest x1 11.8 us: shards(): lax.all_to_all(nbr_keys, 'tp', split_axis=1, concat_axis=0, tiled=True)]
    dot_general x3 -> x0, matrix products: 8.81 us -> none  [the longest x1 7.74 us: shards(): jnp.dot(attn, lax.all_gather(out_weight, 'rows', axis=1, tiled=True), pre...]
    unnamed x8 -> x12, local copies, waits for them, and re-layouts: 1.06 us -> 6.77 us
    all_to_all x2 -> x0, local copies, waits for them, and re-layouts: 4.69 us -> none  [the longest x1 2.39 us: shards(): lax.all_to_all(nbr_values, 'tp', split_axis=1, concat_axis=0, tiled=True)]
  transfers between devices with their start and end apart: 4 -> 0, of which waited for: 4 -> 0; matrix products, arithmetic and copies ran while one was open for 6% -> 0% of each run, Pallas kernels for 0% -> 0%
where the time goes in v1:
time: 100 us
  Pallas kernels  93.4 us (93%)
  local copies, waits for them, and re-layouts  6.77 us (7%)
    pallas_call x1, Pallas kernels, shards(): pl.pallas_call(functools.partial(kernel, do_kv, do_w, do_rs, score_at), o...  93.4 us
    unnamed x12, local copies, waits for them, and re-layouts  6.77 us

profile of v1, /device:TPU:1, one launch (start us, length us, event | category | flops | bytes accessed | tf_op | source)
XLA Modules:
  0.0 100.2 jit_solution(12805611616129704912)
XLA Ops:
  0.0 0.8 copy.7.idx_ref
  0.8 0.0 copy-start
  0.8 1.2 %copy-done = bf16[64,8192]{1,0:T(8,128)(2,1)S(1)} copy-done((bf16[64,8192]{1,0:T(8,128)(2,1)S(1)}, bf16[64,8192]{1,0:T(8,128)(2,1)}, u32[]{:S(2)}) %copy-start) | copy-done | bytes 1048600
  2.0 0.0 copy-start.1
  2.0 1.2 %copy-done.1 = bf16[64,8192]{1,0:T(8,128)(2,1)S(1)} copy-done((bf16[64,8192]{1,0:T(8,128)(2,1)S(1)}, bf16[64,8192]{1,0:T(8,128)(2,1)}, u32[]{:S(2)}) %copy-start.1) | copy-done | bytes 1048600
  3.2 0.0 copy-start.2
  3.2 0.9 copy-done.2
  4.2 0.0 copy-start.3
  4.2 0.9 copy-done.3
  5.1 0.0 copy-start.4
  5.1 0.9 copy-done.4
  6.1 93.4 %shard_map.64 = bf16[16,8192]{1,0:T(8,128)(2,1)S(1)} custom-call(s32[4,2]{1,0:T(4,128)S(1)} %copy.7.idx_ref, bf16[256,512]{1,0:T(8,128)(2,1)S(1)} %copy-done.2, bf16[64,8192]{1,0:T(8,128)(2,1)S(1)} %copy-done, bf16[64,8192]{1,0:T(8,128)(2,1)S(1)} %copy-done.1, bf16[16,8192]{1,0:T(8,128)(2,1)S(1)} %copy-done.3, bf16[512,256]{1,0:T(8,128)(2,1)S(1)} %copy-done.4), custom_call_target="tpu_custom_call" | custom-call | flops 2400000000 | bytes 12000000 | tf_op jit(solution)/shard_map/pallas_call | solution.py:374
  99.5 0.7 copy.9
Async XLA Ops:
  0.8 1.2 %copy-start = (bf16[64,8192]{1,0:T(8,128)(2,1)S(1)}, bf16[64,8192]{1,0:T(8,128)(2,1)}, u32[]{:S(2)}) copy-start(bf16[64,8192]{1,0:T(8,128)(2,1)} %k_ref.1) | copy-start | bytes 3145732
  2.0 1.2 %copy-start.1 = (bf16[64,8192]{1,0:T(8,128)(2,1)S(1)}, bf16[64,8192]{1,0:T(8,128)(2,1)}, u32[]{:S(2)}) copy-start(bf16[64,8192]{1,0:T(8,128)(2,1)} %v_ref.1) | copy-start | bytes 3145732
  3.2 0.9 copy-start.2
  4.2 0.9 copy-start.3
  5.1 0.9 copy-start.4

commit v2 on v1

v2 whole, which is shorter than its diff:
```python
import heapq
import math

import jax
import jax.numpy as jnp
from jax import lax
from jax.experimental import pallas as pl
from jax.experimental.pallas import tpu as pltpu
from jax.sharding import PartitionSpec as P

MESH = pl.DeviceIdType.MESH
F32, BF16 = jnp.float32, jnp.bfloat16

HD, CH, R = 128, 64, 128
NX, NY, NZ = 4, 8, 8
TP, ROWS = 16, 32
TOK, HCOLS, WCOLS, KROWS = 256, 512, 256, 64
D = 8192
SPANS, HEADS = TOK // CH, HCOLS // HD
TOKZ, TOKD = TOK // NZ, TOK // TP
HALF = D // 2
G = 4
GC = HALF // G
GB = GC // WCOLS

PARTS = ((0, 208, 112), (208, 512, 352))

SCORE_AT = 30.0


def gather_plan():
    messages, needs = [], []

    def add(part, axis, sign, dx, dy, piece, need):
        lo, hi, mid = PARTS[part]
        lo, hi = ((lo, hi), (lo, mid), (mid, hi))[piece]
        messages.append((axis, sign, dx, dy, lo, hi))
        needs.append(need)
        return len(messages) - 1

    def ring(part, axis, size, other, need):
        got = {0: need}
        for sign in (1, -1):
            for step in range(size // 2):
                at = -sign * step
                last = step == size // 2 - 1
                piece = 0 if not last else (1 if sign == 1 else 2)
                dx, dy = (at, other) if axis == 0 else (other, at)
                bring = add(part, axis, sign, dx, dy, piece, got[at])
                key = size // 2 if last else at - sign
                got[key] = got.get(key, ()) + (bring,) if last else (bring,)
        return got

    for bx, need in ring(0, 0, NX, 0, ()).items():
        ring(0, 1, NY, bx, need)
    for by, need in ring(1, 1, NY, 0, ()).items():
        ring(1, 0, NX, by, need)

    count = len(messages)
    feeds = [[j for j in range(count) if i in needs[j]] for i in range(count)]
    depth = [0] * count
    for i in reversed(range(count)):
        depth[i] = max([1 + depth[j] for j in feeds[i]], default=0)
    rate, delay = 2 * WCOLS * 2 / 90e3, 1.5
    free = {}
    queue = []
    left = [len(n) for n in needs]

    def launch(i, now):
        axis, sign, _, _, lo, hi = messages[i]
        begin = max(now, free.get((axis, sign), 0.0))
        free[axis, sign] = begin + (hi - lo) * rate
        heapq.heappush(queue, (free[axis, sign] + delay, i))

    first = sorted((i for i in range(count) if not needs[i]), key=lambda i: (-depth[i], i))
    for i in first:
        launch(i, 0.0)
    steps = []
    while queue:
        now, i = heapq.heappop(queue)
        ready = []
        for j in feeds[i]:
            left[j] -= 1
            if left[j] == 0:
                ready.append(j)
        ready.sort(key=lambda j: (-depth[j], j))
        for j in ready:
            launch(j, now)
        steps.append((now, i, ready, not feeds[i]))
    return messages, first, steps


MESSAGES, FIRST, STEPS = gather_plan()


def wrap(axis, d):
    size = (NX, NY)[axis]
    return (d + size // 2 - 1) % size - (size // 2 - 1)


def came(i):
    axis, sign, dx, dy, _, _ = MESSAGES[i]
    return (wrap(0, dx - sign), wrap(1, dy)) if axis == 0 else (wrap(0, dx), wrap(1, dy - sign))


def arrival_order():
    when = {(0, 0): 0.0}
    for now, i, _, _ in STEPS:
        when[came(i)] = now
    return sorted(when, key=lambda at: (when[at], at))


ORDER = arrival_order()


def place(i):
    return ORDER.index(came(i))


def sum_plan():
    project_us, meet_us, small_us, link_us, delay_us = 7.0 / G, 1.6, 0.3, 6.0 / G, 1.6
    now, free = 0.0, 0.0
    ready = []
    order, left = [], list(range(G))
    while left or ready:
        able = sorted((-stage, g) for t, stage, g in ready if t <= now)
        if able:
            stage, g = -able[0][0], able[0][1]
            ready = [r for r in ready if r[1:] != (stage, g)]
            now += small_us
            order.append((1, g, 0) if stage == 0 else (2, g, stage) if stage < 4 else (3, g, 0))
            if stage < 4:
                free = max(now, free) + link_us * (0.5 if stage == 0 else 1.0)
                ready.append((free + delay_us, stage + 1, g))
        elif left:
            g = left.pop(0)
            order.append((0, g, 0))
            ready.append((now + project_us / 2 + meet_us, 0, g))
            now += project_us
        else:
            now = min(t for t, _, _ in ready)
    return order, now


SUMS, SUMS_US = sum_plan()


def kernel(
    idx_hbm, q_ref, k_ref, v_ref, res_ref, w_ref, out_ref,
    idx_ref, kbuf, vbuf, qbuf, rbuf, wbuf, attn, probs, xsend, xrecv, pown, sbuf, shared, chains, ends,
    idx_sem, local_sem, kv_send, kv_recv, w_send, w_recv,
    x_send, x_recv, s_send, s_recv, c_send, c_recv, e_send, e_recv,
):
    row, tp = lax.axis_index("rows"), lax.axis_index("tp")
    x, y = row // NY, row % NY
    z, core = tp // 2, tp % 2
    sibling = z * 2 + (1 - core)

    def at_z(dz, dc=0):
        return ((z + dz) % NZ) * 2 + (core + dc) % 2

    def at_xy(axis, sign):
        if axis == 0:
            return ((x + sign) % NX) * NY + y
        return x * NY + (y + sign) % NY

    partners = [(row, sibling)]
    partners += [(row, at_z(dz, dc)) for dz in (4, 3, -3, 2, -2, 1, -1) for dc in (0, 1)]
    around = [(at_xy(axis, sign), tp) for axis in (0, 1) for sign in (1, -1)]

    barrier = pltpu.get_barrier_semaphore()
    for who in partners + around:
        pl.semaphore_signal(barrier, inc=1, device_id=who, device_id_type=MESH)

    own = (z, pl.ds(pl.multiple_of(core * KROWS, KROWS), KROWS))
    own_cols = pl.multiple_of(tp * HCOLS, HCOLS)

    fetch = pltpu.make_async_copy(idx_hbm, idx_ref, idx_sem)
    fetch.start()
    locals_ = [
        pltpu.make_async_copy(q_ref, qbuf, local_sem.at[0]),
        pltpu.make_async_copy(k_ref.at[:, pl.ds(own_cols, HCOLS)], kbuf.at[own], kv_recv.at[0]),
        pltpu.make_async_copy(v_ref.at[:, pl.ds(own_cols, HCOLS)], vbuf.at[own], kv_recv.at[1]),
        pltpu.make_async_copy(w_ref, wbuf.at[row], local_sem.at[3]),
        pltpu.make_async_copy(res_ref, rbuf, local_sem.at[4]),
    ]
    for copy in locals_:
        copy.start()
    pl.semaphore_wait(barrier, len(partners) + len(around))

    def owner(dx, dy):
        return ((x + dx) % NX) * NY + (y + dy) % NY

    def w_copy(i, arrived):
        axis, sign, dx, dy, lo, hi = MESSAGES[i]
        if arrived:
            dx, dy = (dx - sign, dy) if axis == 0 else (dx, dy - sign)
        slot = wbuf.at[owner(dx, dy), pl.ds(lo, hi - lo), :]
        mine = not arrived and dx == 0 and dy == 0
        return pltpu.make_async_remote_copy(
            src_ref=w_ref.at[pl.ds(lo, hi - lo), :] if mine else slot,
            dst_ref=slot,
            send_sem=w_send,
            recv_sem=w_recv.at[i],
            device_id=(at_xy(axis, sign), tp),
            device_id_type=MESH,
        )

    def send_kv(which):
        src, dst = ((k_ref, kbuf), (v_ref, vbuf))[which]
        for _, to in partners[1:] + partners[:1]:
            pltpu.make_async_remote_copy(
                src_ref=src.at[:, pl.ds(pl.multiple_of(to * HCOLS, HCOLS), HCOLS)],
                dst_ref=dst.at[own],
                send_sem=kv_send.at[which],
                recv_sem=kv_recv.at[which],
                device_id=(row, to),
                device_id_type=MESH,
            ).start()

    for i in FIRST:
        w_copy(i, False).start()
    send_kv(0)
    send_kv(1)
    def kv_wait(which):
        buf = (kbuf, vbuf)[which]
        pltpu.make_async_copy(buf, buf, kv_recv.at[which]).wait()
    def score(span):
        rows = pl.ds(span * CH, CH)
        keys = [kbuf[idx_ref[k, span]] for k in range(2)]
        for h in range(HEADS):
            query = qbuf[rows, h * HD:(h + 1) * HD]
            raw = jnp.concatenate(
                [
                    lax.dot_general(
                        query, block[:, h * HD:(h + 1) * HD], (((1,), (1,)), ((), ())),
                        preferred_element_type=F32,
                    )
                    for block in keys
                ],
                axis=1,
            ) * (1.0 / math.sqrt(HD))
            weights = jnp.exp(raw - jnp.max(raw, axis=1, keepdims=True))
            total = jnp.sum(weights, axis=1, keepdims=True)
            probs[rows, h * 2 * R:(h + 1) * 2 * R] = (weights / total).astype(BF16)

    def attend(span):
        rows = pl.ds(span * CH, CH)
        values = [vbuf[idx_ref[k, span]] for k in range(2)]
        for h in range(HEADS):
            value = jnp.concatenate([block[:, h * HD:(h + 1) * HD] for block in values], axis=0)
            out = jnp.dot(probs[rows, h * 2 * R:(h + 1) * 2 * R], value, preferred_element_type=F32)
            attn[rows, h * HD:(h + 1) * HD] = out.astype(BF16)

    locals_[0].wait()
    fetch.wait()
    scored = False
    late = []
    for now, i, sends, last in STEPS:
        if now > SCORE_AT and not scored:
            scored = True
            kv_wait(0)
            for span in range(SPANS):
                score(span)
        if last:
            late.append(i)
            continue
        w_copy(i, True).wait_recv()
        for j in sends:
            w_copy(j, False).start()
    if not scored:
        kv_wait(0)
        for span in range(SPANS):
            score(span)
    kv_wait(1)
    for span in range(SPANS):
        attend(span)
    for copy in locals_[3:]:
        copy.wait()

    def block_of(side, g, j):
        (ax, ay), (bx, by) = (ORDER[(g * 2 + s) * GB + j] for s in range(2))
        return owner(ax + side * (bx - ax), ay + side * (by - ay))

    def arrived(g):
        for i in late:
            if place(i) // (2 * GB) == g:
                w_copy(i, True).wait_recv()

    def tokens_of(dz, rows=TOKZ, base=0):
        return pl.ds(pl.multiple_of(((z + dz) % NZ) * TOKZ + base, rows), rows)

    def remote(src, dst, send, recv, to):
        return pltpu.make_async_remote_copy(
            src_ref=src, dst_ref=dst, send_sem=send, recv_sem=recv, device_id=(row, to), device_id_type=MESH
        )

    def chain(g, step, way):
        buf = chains.at[way, g]
        if step == 0:
            cols = pl.ds(way * (GC // 2), GC // 2)
            src, dst = sbuf.at[g, tokens_of(4), cols], buf.at[0, :, cols]
        else:
            src, dst = buf.at[step - 1], buf.at[step]
        return remote(src, dst, c_send.at[way, g, step], c_recv.at[way, g, step], at_z(1 - 2 * way))

    def last_hop(g, way, dc):
        rows = pl.ds(pl.multiple_of(((core + dc) % 2) * TOKD, TOKD), TOKD)
        return remote(
            chains.at[way, g, 2, rows], ends.at[way, dc, g],
            e_send.at[way, dc, g], e_recv.at[way, dc, g], at_z(1 - 2 * way, dc),
        )

    def exchange(g):
        return remote(xsend.at[g], xrecv.at[g], x_send.at[g], x_recv.at[g], sibling)

    def share(g):
        src = sbuf.at[g, tokens_of(0, TOKD, (1 - core) * TOKD)]
        return remote(src, shared.at[g], s_send.at[g], s_recv.at[g], sibling)

    def project(g):
        arrived(g)
        for other in (True, False):
            side = 1 - core if other else core
            for j in range(GB):
                part = jnp.dot(attn[...], wbuf[block_of(side, g, j)], preferred_element_type=F32)
                cols = slice(j * WCOLS, (j + 1) * WCOLS)
                if other:
                    xsend[g, :, cols] = part.astype(BF16)
                else:
                    pown[g, :, cols] = part
            if other:
                exchange(g).start()

    def combine(g):
        exchange(g).wait_recv()
        sbuf[g] = (pown[g] + xrecv[g].astype(F32)).astype(BF16)
        for way in range(2):
            chain(g, 0, way).start()
        share(g).start()

    def relay(g, step):
        for way in range(2):
            chain(g, step - 1, way).wait_recv()
            buf = chains.at[way, g, step - 1]
            tokens = tokens_of((1 - 2 * way) * (4 - step))
            if step == 1:
                cut = GC // 2
                got, rest = slice(way * cut, (way + 1) * cut), slice((1 - way) * cut, (2 - way) * cut)
                buf[:, got] = (buf[:, got].astype(F32) + sbuf[g, tokens, got].astype(F32)).astype(BF16)
                buf[:, rest] = sbuf[g, tokens, rest]
            else:
                buf[...] = (buf[...].astype(F32) + sbuf[g, tokens, :].astype(F32)).astype(BF16)
            if step < 3:
                chain(g, step, way).start()
            else:
                for dc in (1, 0):
                    last_hop(g, way, dc).start()

    def finish(g):
        share(g).wait_recv()
        for way in range(2):
            for dc in range(2):
                last_hop(g, way, dc).wait_recv()
        mine = tokens_of(0, TOKD, core * TOKD)
        for dc in range(2):
            side = core if dc == 0 else 1 - core
            for j in range(GB):
                at = pl.ds(pl.multiple_of(block_of(side, g, j) * WCOLS, WCOLS), WCOLS)
                cols = slice(j * WCOLS, (j + 1) * WCOLS)
                here = sbuf[g, mine, cols] if dc == 0 else shared[g, :, cols]
                out_ref[:, at] = (
                    rbuf[:, at].astype(F32)
                    + here.astype(F32)
                    + ends[0, dc, g, :, cols].astype(F32)
                    + ends[1, dc, g, :, cols].astype(F32)
                ).astype(BF16)

    for what, g, step in SUMS:
        if what == 0:
            project(g)
        elif what == 1:
            combine(g)
        elif what == 2:
            relay(g, step)
        else:
            finish(g)
    for g in range(G):
        exchange(g).wait_send()
        share(g).wait_send()
        for way in range(2):
            for step in range(3):
                chain(g, step, way).wait_send()
            for dc in range(2):
                last_hop(g, way, dc).wait_send()
    waitbuf = wbuf.at[pl.ds(0, TP - 1), pl.ds(0, KROWS * HCOLS // WCOLS), :]
    for which in range(2):
        pltpu.make_async_copy(waitbuf, waitbuf, kv_send.at[which]).wait()
    rest = wbuf.at[pl.ds(0, ROWS - 1)]
    pltpu.make_async_copy(rest, rest, w_send).wait()


def solution(mesh):
    def shards(queries, nbr_keys, nbr_values, nbr_index, residual, out_weight):
        hbm = pl.BlockSpec(memory_space=pl.ANY)
        dma = pltpu.SemaphoreType.DMA
        return pl.pallas_call(
            kernel,
            out_shape=jax.ShapeDtypeStruct((TOKD, D), BF16),
            in_specs=[hbm] * 6,
            out_specs=pl.BlockSpec(memory_space=pltpu.VMEM),
            scratch_shapes=[
                pltpu.SMEM((2, SPANS), jnp.int32),
                pltpu.VMEM((NZ, R, HCOLS), BF16),
                pltpu.VMEM((NZ, R, HCOLS), BF16),
                pltpu.VMEM((TOK, HCOLS), BF16),
                pltpu.VMEM((TOKD, D), BF16),
                pltpu.VMEM((ROWS, HCOLS, WCOLS), BF16),
                pltpu.VMEM((TOK, HCOLS), BF16),
                pltpu.VMEM((TOK, HEADS * 2 * R), BF16),
                pltpu.VMEM((G, TOK, GC), BF16),
                pltpu.VMEM((G, TOK, GC), BF16),
                pltpu.VMEM((G, TOK, GC), F32),
                pltpu.VMEM((G, TOK, GC), BF16),
                pltpu.VMEM((G, TOKD, GC), BF16),
                pltpu.VMEM((2, G, 3, TOKZ, GC), BF16),
                pltpu.VMEM((2, 2, G, TOKD, GC), BF16),
                dma, dma((5,)), dma((2,)), dma((2,)), dma, dma((len(MESSAGES),)),
                dma((G,)), dma((G,)), dma((G,)), dma((G,)),
                dma((2, G, 3)), dma((2, G, 3)), dma((2, 2, G)), dma((2, 2, G)),
            ],
            compiler_params=pltpu.CompilerParams(
                collective_id=0, has_side_effects=True, vmem_limit_bytes=56 * 1024 * 1024
            ),
            cost_estimate=pl.CostEstimate(flops=2_400_000_000, bytes_accessed=12_000_000, transcendentals=262144),
        )(nbr_index.T, queries, nbr_keys, nbr_values, residual, out_weight)

    placed = (
        P("rows", "tp"),
        P(("rows", "tp"), None),
        P(("rows", "tp"), None),
        P("rows", None),
        P(("rows", "tp"), None),
        P("tp", "rows"),
    )
    return jax.shard_map(
        shards, mesh=mesh, in_specs=placed, out_specs=P(("rows", "tp"), None), check_vma=False
    )
```

time: 100 us -> 90.8 us (0.908)
  local copies, waits for them, and re-layouts: 6.77 us -> 1.67 us
  Pallas kernels: 93.4 us -> 89 us
    unnamed x12 -> x1, local copies, waits for them, and re-layouts: 6.77 us -> 1.67 us
    pallas_call x1, Pallas kernels: 93.4 us -> 89 us  [shards(): pl.pallas_call(kernel, out_shape=jax.ShapeDtypeStruct((TOKD, D), BF16), i...]
where the time goes in v2:
time: 90.8 us; the launch traced here: 90.7 us
  Pallas kernels  89 us (98%)
  local copies, waits for them, and re-layouts  1.67 us (2%)
    pallas_call x1, Pallas kernels, shards(): pl.pallas_call(kernel, out_shape=jax.ShapeDtypeStruct((TOKD, D), BF16), i...  89 us

profile of v2, /device:TPU:1, one launch (start us, length us, event | category | flops | bytes accessed | tf_op | source)
XLA Modules:
  0.0 90.7 jit_solution(9578999916817527451)
XLA Ops:
  0.0 89.0 %shard_map.64 = bf16[16,8192]{1,0:T(8,128)(2,1)} custom-call(s32[2,4]{1,0:T(2,128)} %bitcast.1, bf16[256,512]{1,0:T(8,128)(2,1)} %q_ref.1, bf16[64,8192]{1,0:T(8,128)(2,1)} %k_ref.1, bf16[64,8192]{1,0:T(8,128)(2,1)} %v_ref.1, bf16[16,8192]{1,0:T(8,128)(2,1)} %res_ref.1, bf16[512,256]{1,0:T(8,128)(2,1)} %w_ref.1), custom_call_target="tpu_custom_call" | custom-call | flops 2400000000 | bytes 12000000 | tf_op jit(solution)/shard_map/pallas_call | solution.py:407
  89.0 1.7 %copy.8 = bf16[16,8192]{1,0:T(8,128)(2,1)} copy(bf16[16,8192]{1,0:T(8,128)(2,1)} %shard_map.64) | data formatting | bytes 524288

commit v3 on v2

--- a/solution.py
+++ b/solution.py
@@ -22,6 +22,8 @@
 G = 4
 GC = HALF // G
 GB = GC // WCOLS
+
+PIECES = ((4,), (3, -3, 2, -2), (1, -1, 0))
 
 PARTS = ((0, 208, 112), (208, 512, 352))
 
@@ -113,12 +115,30 @@
 ORDER = arrival_order()
 
 
-def place(i):
-    return ORDER.index(came(i))
+def turns():
+    passed = [(now, i, sends) for now, i, sends, last in STEPS if not last]
+    chunk = {i: ORDER.index(came(i)) // (2 * GB) for _, i, _, _ in STEPS}
+    signal = {i: n for n, (_, i, _) in enumerate(passed)}
+    sizes, own = [], len(passed) + G
+    for g in range(G):
+        rest, alone, fits = [i for _, i, _, last in STEPS if last and chunk[i] == g], [], []
+        while rest and not fits:
+            total = sum(MESSAGES[i][5] - MESSAGES[i][4] for i in rest)
+            fits = [k for k in range(1, ROWS) if total % (16 * k) == 0 and total // k <= HCOLS]
+            if not fits:
+                alone.append(rest.pop())
+        signal.update({i: len(passed) + g for i in rest})
+        signal.update({i: own + n for n, i in enumerate(alone)})
+        own += len(alone)
+        sizes.append(((fits[0], total // fits[0]) if rest else None, alone))
+    return passed, signal, sizes, own
+
+
+TURNS, SIGNAL, LATE, W_SEMS = turns()
 
 
 def sum_plan():
-    project_us, meet_us, small_us, link_us, delay_us = 7.0 / G, 1.6, 0.3, 6.0 / G, 1.6
+    project_us, meet_us, small_us, link_us, delay_us = 2.4 / G, 1.3, 0.25, 5.8 / G, 1.6
     now, free = 0.0, 0.0
     ready = []
     order, left = [], list(range(G))
@@ -147,7 +167,7 @@
 
 def kernel(
     idx_hbm, q_ref, k_ref, v_ref, res_ref, w_ref, out_ref,
-    idx_ref, kbuf, vbuf, qbuf, rbuf, wbuf, attn, probs, xsend, xrecv, pown, sbuf, shared, chains, ends,
+    idx_ref, kbuf, vbuf, qbuf, rbuf, wbuf, attn, probs, xsend, xrecv, pown, first, last, shared, chains, ends,
     idx_sem, local_sem, kv_send, kv_recv, w_send, w_recv,
     x_send, x_recv, s_send, s_recv, c_send, c_recv, e_send, e_recv,
 ):
@@ -201,7 +221,7 @@
             src_ref=w_ref.at[pl.ds(lo, hi - lo), :] if mine else slot,
             dst_ref=slot,
             send_sem=w_send,
-            recv_sem=w_recv.at[i],
+            recv_sem=w_recv.at[SIGNAL[i]],
             device_id=(at_xy(axis, sign), tp),
             device_id_type=MESH,
         )
@@ -254,24 +274,22 @@
 
     locals_[0].wait()
     fetch.wait()
-    scored = False
-    late = []
-    for now, i, sends, last in STEPS:
-        if now > SCORE_AT and not scored:
-            scored = True
-            kv_wait(0)
-            for span in range(SPANS):
-                score(span)
-        if last:
-            late.append(i)
-            continue
-        w_copy(i, True).wait_recv()
-        for j in sends:
-            w_copy(j, False).start()
-    if not scored:
-        kv_wait(0)
-        for span in range(SPANS):
-            score(span)
+    turn = 0
+
+    def pump(until):
+        nonlocal turn
+        while turn < len(TURNS) and TURNS[turn][0] < until:
+            _, i, sends = TURNS[turn]
+            w_copy(i, True).wait_recv()
+            for j in sends:
+                w_copy(j, False).start()
+            turn += 1
+
+    pump(SCORE_AT)
+    kv_wait(0)
+    for span in range(SPANS):
+        score(span)
+    pump(math.inf)
     kv_wait(1)
     for span in range(SPANS):
         attend(span)
@@ -283,9 +301,13 @@
         return owner(ax + side * (bx - ax), ay + side * (by - ay))
 
     def arrived(g):
-        for i in late:
-            if place(i) // (2 * GB) == g:
-                w_copy(i, True).wait_recv()
+        shared_size, alone = LATE[g]
+        for i in alone:
+            w_copy(i, True).wait_recv()
+        if shared_size:
+            count, rows = shared_size
+            part = wbuf.at[pl.ds(0, count), pl.ds(0, rows), :]
+            pltpu.make_async_copy(part, part, w_recv.at[len(TURNS) + g]).wait()
 
     def tokens_of(dz, rows=TOKZ, base=0):
         return pl.ds(pl.multiple_of(((z + dz) % NZ) * TOKZ + base, rows), rows)
@@ -299,24 +321,32 @@
         buf = chains.at[way, g]
         if step == 0:
             cols = pl.ds(way * (GC // 2), GC // 2)
-            src, dst = sbuf.at[g, tokens_of(4), cols], buf.at[0, :, cols]
+            src, dst = first.at[g, :, cols], buf.at[0, :, cols]
         else:
             src, dst = buf.at[step - 1], buf.at[step]
-        return remote(src, dst, c_send.at[way, g, step], c_recv.at[way, g, step], at_z(1 - 2 * way))
+        return remote(src, dst, c_send, c_recv.at[way, g, step], at_z(1 - 2 * way))
 
     def last_hop(g, way, dc):
         rows = pl.ds(pl.multiple_of(((core + dc) % 2) * TOKD, TOKD), TOKD)
         return remote(
-            chains.at[way, g, 2, rows], ends.at[way, dc, g],
-            e_send.at[way, dc, g], e_recv.at[way, dc, g], at_z(1 - 2 * way, dc),
+            chains.at[way, g, 2, rows], ends.at[g, way, dc],
+            e_send, e_recv.at[g], at_z(1 - 2 * way, dc),
         )
 
-    def exchange(g):
-        return remote(xsend.at[g], xrecv.at[g], x_send.at[g], x_recv.at[g], sibling)
+    def exchange(g, piece):
+        for dz in PIECES[piece]:
+            rows = tokens_of(dz)
+            remote(xsend.at[g, rows], xrecv.at[g, rows], x_send, x_recv.at[g, piece], sibling).start()
+
+    def met(g, piece):
+        part = xrecv.at[g, pl.ds(0, len(PIECES[piece]) * TOKZ)]
+        pltpu.make_async_copy(part, part, x_recv.at[g, piece]).wait()
+
+    def both(g, rows, cols=slice(None)):
+        return pown[g, rows, cols] + xrecv[g, rows, cols].astype(F32)
 
     def share(g):
-        src = sbuf.at[g, tokens_of(0, TOKD, (1 - core) * TOKD)]
-        return remote(src, shared.at[g], s_send.at[g], s_recv.at[g], sibling)
+        return remote(last.at[g], shared.at[g], s_send, s_recv.at[g], sibling)
 
     def project(g):
         arrived(g)
@@ -330,16 +360,19 @@
                 else:
                     pown[g, :, cols] = part
             if other:
-                exchange(g).start()
-
-    def combine(g):
-        exchange(g).wait_recv()
-        sbuf[g] = (pown[g] + xrecv[g].astype(F32)).astype(BF16)
+                exchange(g, 0)
+
+    def start(g):
+        met(g, 0)
+        first[g] = both(g, tokens_of(4)).astype(BF16)
         for way in range(2):
             chain(g, 0, way).start()
-        share(g).start()
+        exchange(g, 1)
+        exchange(g, 2)
 
     def relay(g, step):
+        if step != 2:
+            met(g, 1 if step == 1 else 2)
         for way in range(2):
             chain(g, step - 1, way).wait_recv()
             buf = chains.at[way, g, step - 1]
@@ -347,52 +380,48 @@
             if step == 1:
                 cut = GC // 2
                 got, rest = slice(way * cut, (way + 1) * cut), slice((1 - way) * cut, (2 - way) * cut)
-                buf[:, got] = (buf[:, got].astype(F32) + sbuf[g, tokens, got].astype(F32)).astype(BF16)
-                buf[:, rest] = sbuf[g, tokens, rest]
+                buf[:, got] = (buf[:, got].astype(F32) + both(g, tokens, got)).astype(BF16)
+                buf[:, rest] = both(g, tokens, rest).astype(BF16)
             else:
-                buf[...] = (buf[...].astype(F32) + sbuf[g, tokens, :].astype(F32)).astype(BF16)
+                buf[...] = (buf[...].astype(F32) + both(g, tokens)).astype(BF16)
             if step < 3:
                 chain(g, step, way).start()
             else:
                 for dc in (1, 0):
                     last_hop(g, way, dc).start()
+        if step == 3:
+            last[g] = both(g, tokens_of(0, TOKD, (1 - core) * TOKD)).astype(BF16)
+            share(g).start()
 
     def finish(g):
         share(g).wait_recv()
-        for way in range(2):
-            for dc in range(2):
-                last_hop(g, way, dc).wait_recv()
+        pltpu.make_async_copy(ends.at[g], ends.at[g], e_recv.at[g]).wait()
         mine = tokens_of(0, TOKD, core * TOKD)
         for dc in range(2):
             side = core if dc == 0 else 1 - core
             for j in range(GB):
                 at = pl.ds(pl.multiple_of(block_of(side, g, j) * WCOLS, WCOLS), WCOLS)
                 cols = slice(j * WCOLS, (j + 1) * WCOLS)
-                here = sbuf[g, mine, cols] if dc == 0 else shared[g, :, cols]
+                here = both(g, mine, cols) if dc == 0 else shared[g, :, cols].astype(F32)
                 out_ref[:, at] = (
                     rbuf[:, at].astype(F32)
-                    + here.astype(F32)
-                    + ends[0, dc, g, :, cols].astype(F32)
-                    + ends[1, dc, g, :, cols].astype(F32)
+                    + here
+                    + ends[g, 0, dc, :, cols].astype(F32)
+                    + ends[g, 1, dc, :, cols].astype(F32)
                 ).astype(BF16)
 
     for what, g, step in SUMS:
         if what == 0:
             project(g)
         elif what == 1:
-            combine(g)
+            start(g)
         elif what == 2:
             relay(g, step)
         else:
             finish(g)
-    for g in range(G):
-        exchange(g).wait_send()
-        share(g).wait_send()
-        for way in range(2):
-            for step in range(3):
-                chain(g, step, way).wait_send()
-            for dc in range(2):
-                last_hop(g, way, dc).wait_send()
+    sent = wbuf.at[pl.ds(0, 2 * G * 5 * GB * TOKZ // 2 // HCOLS)]
+    for part, sem in ((xsend, x_send), (shared, s_send), (ends, e_send), (sent, c_send)):
+        pltpu.make_async_copy(part, part, sem).wait()
     waitbuf = wbuf.at[pl.ds(0, TP - 1), pl.ds(0, KROWS * HCOLS // WCOLS), :]
     for which in range(2):
         pltpu.make_async_copy(waitbuf, waitbuf, kv_send.at[which]).wait()
@@ -421,13 +450,13 @@
                 pltpu.VMEM((G, TOK, GC), BF16),
                 pltpu.VMEM((G, TOK, GC), BF16),
                 pltpu.VMEM((G, TOK, GC), F32),
-                pltpu.VMEM((G, TOK, GC), BF16),
+                pltpu.VMEM((G, TOKZ, GC), BF16),
+                pltpu.VMEM((G, TOKD, GC), BF16),
                 pltpu.VMEM((G, TOKD, GC), BF16),
                 pltpu.VMEM((2, G, 3, TOKZ, GC), BF16),
-                pltpu.VMEM((2, 2, G, TOKD, GC), BF16),
-                dma, dma((5,)), dma((2,)), dma((2,)), dma, dma((len(MESSAGES),)),
-                dma((G,)), dma((G,)), dma((G,)), dma((G,)),
-                dma((2, G, 3)), dma((2, G, 3)), dma((2, 2, G)), dma((2, 2, G)),
+                pltpu.VMEM((G, 2, 2, TOKD, GC), BF16),
+                dma, dma((5,)), dma((2,)), dma((2,)), dma, dma((W_SEMS,)),
+                dma, dma((G, len(PIECES))), dma, dma((G,)), dma, dma((2, G, 3)), dma, dma((G,)),
             ],
             compiler_params=pltpu.CompilerParams(
                 collective_id=0, has_side_effects=True, vmem_limit_bytes=56 * 1024 * 1024

time: 90.8 us -> 87.8 us (0.967)
  Pallas kernels: 89 us -> 86 us
    pallas_call x1, Pallas kernels: 89 us -> 86 us  [shards(): pl.pallas_call(kernel, out_shape=jax.ShapeDtypeStruct((TOKD, D), BF16), i...]
where the time goes in v3:
time: 87.8 us; the launch traced here: 87.6 us
  Pallas kernels  86 us (98%)
  local copies, waits for them, and re-layouts  1.67 us (2%)
    pallas_call x1, Pallas kernels, shards(): pl.pallas_call(kernel, out_shape=jax.ShapeDtypeStruct((TOKD, D), BF16), i...  86 us

profile of v3, /device:TPU:1, one launch (start us, length us, event | category | flops | bytes accessed | tf_op | source)
XLA Modules:
  0.0 87.6 jit_solution(10919932333014272725)
XLA Ops:
  0.0 86.0 %shard_map.64 = bf16[16,8192]{1,0:T(8,128)(2,1)} custom-call(s32[2,4]{1,0:T(2,128)} %bitcast.1, bf16[256,512]{1,0:T(8,128)(2,1)} %q_ref.1, bf16[64,8192]{1,0:T(8,128)(2,1)} %k_ref.1, bf16[64,8192]{1,0:T(8,128)(2,1)} %v_ref.1, bf16[16,8192]{1,0:T(8,128)(2,1)} %res_ref.1, bf16[512,256]{1,0:T(8,128)(2,1)} %w_ref.1), custom_call_target="tpu_custom_call" | custom-call | flops 2400000000 | bytes 12000000 | tf_op jit(solution)/shard_map/pallas_call | solution.py:436
  86.0 1.7 %copy.8 = bf16[16,8192]{1,0:T(8,128)(2,1)} copy(bf16[16,8192]{1,0:T(8,128)(2,1)} %shard_map.64) | data formatting | bytes 524288

commit v4 on v3

--- a/solution.py
+++ b/solution.py
@@ -23,11 +23,13 @@
 GC = HALF // G
 GB = GC // WCOLS
 
+SCORE_STEP = 1.5
+
 PIECES = ((4,), (3, -3, 2, -2), (1, -1, 0))
 
 PARTS = ((0, 208, 112), (208, 512, 352))
 
-SCORE_AT = 30.0
+SCORE_AT = 36.0
 
 
 def gather_plan():
@@ -289,6 +291,7 @@
     kv_wait(0)
     for span in range(SPANS):
         score(span)
+        pump(SCORE_AT + SCORE_STEP * (span + 1))
     pump(math.inf)
     kv_wait(1)
     for span in range(SPANS):

time: 87.8 us -> 87.8 us (level)
  no operation moved by 1% of the time
where the time goes in v4:
time: 87.8 us; the launch traced here: 87.6 us
  Pallas kernels  86 us (98%)
  local copies, waits for them, and re-layouts  1.67 us (2%)
    pallas_call x1, Pallas kernels, shards(): pl.pallas_call(kernel, out_shape=jax.ShapeDtypeStruct((TOKD, D), BF16), i...  86 us

profile of v4, /device:TPU:1, one launch (start us, length us, event | category | flops | bytes accessed | tf_op | source)
XLA Modules:
  0.0 87.6 jit_solution(7898486537075239143)
XLA Ops:
  0.0 86.0 %shard_map.64 = bf16[16,8192]{1,0:T(8,128)(2,1)} custom-call(s32[2,4]{1,0:T(2,128)} %bitcast.1, bf16[256,512]{1,0:T(8,128)(2,1)} %q_ref.1, bf16[64,8192]{1,0:T(8,128)(2,1)} %k_ref.1, bf16[64,8192]{1,0:T(8,128)(2,1)} %v_ref.1, bf16[16,8192]{1,0:T(8,128)(2,1)} %res_ref.1, bf16[512,256]{1,0:T(8,128)(2,1)} %w_ref.1), custom_call_target="tpu_custom_call" | custom-call | flops 2400000000 | bytes 12000000 | tf_op jit(solution)/shard_map/pallas_call | solution.py:439
  86.0 1.7 %copy.8 = bf16[16,8192]{1,0:T(8,128)(2,1)} copy(bf16[16,8192]{1,0:T(8,128)(2,1)} %shard_map.64) | data formatting | bytes 524288

commit v5 on v4

--- a/solution.py
+++ b/solution.py
@@ -364,13 +364,13 @@
                     pown[g, :, cols] = part
             if other:
                 exchange(g, 0)
+        exchange(g, 1)
 
     def start(g):
         met(g, 0)
         first[g] = both(g, tokens_of(4)).astype(BF16)
         for way in range(2):
             chain(g, 0, way).start()
-        exchange(g, 1)
         exchange(g, 2)
 
     def relay(g, step):

time: 87.8 us -> 87.8 us (level)
  no operation moved by 1% of the time
where the time goes in v5:
time: 87.8 us; the launch traced here: 87.7 us
  Pallas kernels  86 us (98%)
  local copies, waits for them, and re-layouts  1.67 us (2%)
    pallas_call x1, Pallas kernels, shards(): pl.pallas_call(kernel, out_shape=jax.ShapeDtypeStruct((TOKD, D), BF16), i...  86 us

profile of v5, /device:TPU:1, one launch (start us, length us, event | category | flops | bytes accessed | tf_op | source)
XLA Modules:
  0.0 87.7 jit_solution(10340611067860650727)
XLA Ops:
  0.0 86.0 %shard_map.64 = bf16[16,8192]{1,0:T(8,128)(2,1)} custom-call(s32[2,4]{1,0:T(2,128)} %bitcast.1, bf16[256,512]{1,0:T(8,128)(2,1)} %q_ref.1, bf16[64,8192]{1,0:T(8,128)(2,1)} %k_ref.1, bf16[64,8192]{1,0:T(8,128)(2,1)} %v_ref.1, bf16[16,8192]{1,0:T(8,128)(2,1)} %res_ref.1, bf16[512,256]{1,0:T(8,128)(2,1)} %w_ref.1), custom_call_target="tpu_custom_call" | custom-call | flops 2400000000 | bytes 12000000 | tf_op jit(solution)/shard_map/pallas_call | solution.py:439
  86.0 1.7 %copy.8 = bf16[16,8192]{1,0:T(8,128)(2,1)} copy(bf16[16,8192]{1,0:T(8,128)(2,1)} %shard_map.64) | data formatting | bytes 524288
